TPU v7x, 1024 devices: a whole 8x8x8 slice. The times are simulated.
1024 devices in a mesh: dp: 128 (over x_lo, z, y), mp: 8 (over x_hi, core).
Axes of the slice: x: 8 (x_hi: 4, x_lo: 2; x = x_hi * 2 + x_lo), y: 8, z: 8, core: 2. Of those that a mesh axis runs over, the one named last changes fastest.
Arguments:
- activations: bfloat16 [2, 14336, 8192], P(None, 'dp'), may hold values from -24 to 24
- cotangent: bfloat16 [2, 14336, 28672], P(None, 'dp', 'mp'), may hold values from -0.09375 to 0.09375
- subspace_basis: bfloat16 [28672, 512], P('mp'), may hold values from -0.046875 to 0.046875
- weight: bfloat16 [8192, 28672], P('dp', 'mp'), may hold values from -0.0625 to 0.0625
- moment: float32 [8192, 512], P('dp', 'mp'), may hold values from -2 to 2
- second: float32 [8192, 512], P('dp', 'mp'), may hold values from 0.25 to 4
Outputs:
- weight_new: bfloat16 [8192, 28672], P('dp', 'mp')
- moment_new: float32 [8192, 512], P('dp', 'mp')
- second_new: float32 [8192, 512], P('dp', 'mp')
All inputs are finite; a program needn't handle non-finite values.
Results may differ from a plain program's by a relative error of at most 0.006.
Values may be sent and summed in bfloat16 or wider, within the bound.
A program may use at most 32 MiB of HBM per device.

v0:
```python
import jax
import jax.numpy as jnp
from jax import lax
from jax.sharding import PartitionSpec as P

beta_first = 0.9
beta_second = 0.999
epsilon = 1e-08
step_size = 0.25


def shards(activations, cotangent, subspace_basis, weight, moment, second):
    micro_count = activations.shape[0]
    coord_rows = moment.shape[1]
    owned_rows = weight.shape[0]

    def local_rows(number, projected):
        part = activations[number]
        return lax.dot_general(
            part, projected, (((0,), (1,)), ((), ())), preferred_element_type=jnp.float32
        )

    gradient = jnp.zeros((owned_rows, coord_rows), jnp.float32)
    for number in range(micro_count):
        summed = lax.psum_scatter(
            lax.dot_general(
                subspace_basis,
                cotangent[number],
                (((0,), (1,)), ((), ())),
                preferred_element_type=jnp.float32,
            ),
            "mp",
            scatter_dimension=0,
            tiled=True,
        )
        projected = summed.astype(jnp.bfloat16)

        def gradient_term(start, count, number=number, projected=projected):
            return local_rows(number, projected)

        gradient = gradient + lax.psum_scatter(
            gradient_term(jnp.int32(0), lax.axis_size("dp") * owned_rows),
            "dp",
            scatter_dimension=0,
            tiled=True,
        )
    moment_new = beta_first * moment + (1.0 - beta_first) * gradient
    second_new = beta_second * second + (1.0 - beta_second) * gradient * gradient
    direction = (moment_new / (jnp.sqrt(second_new) + epsilon)).astype(jnp.bfloat16)
    update = lax.dot_general(
        lax.all_gather(direction, "mp", axis=1, tiled=True),
        subspace_basis,
        (((1,), (1,)), ((), ())),
        preferred_element_type=jnp.float32,
    )
    weight_new = (weight.astype(jnp.float32) - step_size * update).astype(jnp.bfloat16)
    return (weight_new, moment_new, second_new)


def solution(mesh):
    in_specs = (
        P(None, "dp", None),
        P(None, "dp", "mp"),
        P("mp", None),
        P("dp", "mp"),
        P("dp", "mp"),
        P("dp", "mp"),
    )
    out_specs = (P("dp", "mp"), P("dp", "mp"), P("dp", "mp"))
    return jax.shard_map(shards, mesh=mesh, in_specs=in_specs, out_specs=out_specs, check_vma=False)
```

profile of v0, /device:TPU:1, one launch (start us, length us, event | category | flops | bytes accessed | tf_op | source)
XLA Modules:
  0.0 776.2 jit_solution(2886763469535343744)
XLA Ops:
  7.2 0.0 copy-start.3
  7.2 0.0 reduce-scatter.6.cloned.1.call-start
  7.2 4.2 fusion.10
  11.4 0.0 reduce-scatter.6.cloned.1.call-update
  11.5 0.0 reduce-scatter.8.cloned.1.call-start
  11.5 0.0 copy-done.3
  11.5 3.9 fusion.8
  15.4 0.0 reduce-scatter.8.cloned.1.call-update
  15.4 0.0 reduce-scatter.10.cloned.1.call-start
  15.5 49.8 %reduce-scatter.6.cloned.1.call-done = f32[64,112]{1,0:T(8,128)} async-done(((f32[512,112]{1,0:T(8,128)}), f32[64,112]{1,0:T(8,128)}) %reduce-scatter.6.cloned.1.call-update) | async-done | bytes 28688 | tf_op jit(solution)/shard_map/reduce_scatter | solution.py:25
  65.2 3.3 fusion.4
  68.5 41.6 %reduce-scatter.8.cloned.1.call-done = f32[64,112]{1,0:T(8,128)} async-done(((f32[512,112]{1,0:T(8,128)}), f32[64,112]{1,0:T(8,128)}) %reduce-scatter.8.cloned.1.call-update) | async-done | bytes 28688 | tf_op jit(solution)/shard_map/reduce_scatter | solution.py:25
  110.1 2.6 fusion
  112.7 2.7 copy.17
  115.4 0.0 copy-start.1
  115.4 0.0 copy-start.2
  115.4 0.0 copy-start
  115.4 0.0 reduce-scatter.10.cloned.1.call-update
  115.5 0.7 copy-done.1
  116.2 0.1 copy.13
  116.3 0.0 copy-done.2
  116.3 0.1 copy.14
  116.3 529.1 %reduce-scatter.10.cloned.1.call-done = f32[64,64]{1,0:T(8,128)} async-done(((f32[8192,64]{1,0:T(8,128)}), f32[64,64]{1,0:T(8,128)}) %reduce-scatter.10.cloned.1.call-update) | async-done | bytes 16400
  645.4 0.8 copy.18
  646.3 117.9 %all_gather.3 = bf16[64,512]{0,1:T(8,128)(2,1)S(1)} all-gather(bf16[64,64]{0,1:T(8,128)(2,1)S(1)} %get-tuple-element.9), channel_id=1, replica_groups=mesh['dp'=128,'mp'=8] {'mp'}, dimensions={1}, use_global_device_ids=true | all-gather | bytes 73728 | tf_op jit(solution)/shard_map/all_gather | solution.py:51
  764.2 0.7 copy.15
  764.9 0.7 copy.16
  765.6 0.0 copy-done
  765.6 4.0 fusion.2
  (1 shorter events, 0.0 us)
Async XLA Ops:
  7.2 4.3 copy-start.3
  7.2 58.1 %reduce-scatter.6.cloned.1.call-start = ((), (), s32[]{:S(2)}) async-start(), calls=%async_computation.3 | async-start | bytes 294912 | tf_op jit(solution)/shard_map/reduce_scatter | solution.py:25
  11.5 98.7 %reduce-scatter.8.cloned.1.call-start = ((), (), s32[]{:S(2)}) async-start(), calls=%async_computation.4 | async-start | bytes 294912 | tf_op jit(solution)/shard_map/reduce_scatter | solution.py:25
  15.4 630.0 %reduce-scatter.10.cloned.1.call-start = ((), (), s32[]{:S(2)}) async-start(), calls=%async_computation.5 | async-start | bytes 4227072
  115.4 0.8 copy-start.1
  115.4 0.8 copy-start.2
  115.4 650.2 %copy-start = (bf16[64,3584]{1,0:T(8,128)(2,1)S(1)}, bf16[64,3584]{1,0:T(8,128)(2,1)}, u32[]{:S(2)}) copy-start(bf16[64,3584]{1,0:T(8,128)(2,1)} %param.9) | copy-start | bytes 1376260
Sparse Core Ops, SparseCore 0:
  12.0 53.2 reduce-scatter.5
  69.0 41.0 reduce-scatter.7
  115.6 529.8 reduce-scatter.9
where the time goes:
time: 776 us
  waiting for transfers between devices  620 us (80%)
  blocking collectives  118 us (15%)
  matrix products  18 us (2%)
  between operations  13.8 us (2%)
    unnamed x4, waiting for transfers between devices  529 us
    all_gather x1, blocking collectives, shards(): lax.all_gather(direction, 'mp', axis=1, tiled=True)  118 us
    reduce_scatter x2, waiting for transfers between devices, shards(): lax.psum_scatter(lax.dot_general(subspace_basis, cotangent[number], (((0,...  91.4 us
  transfers between devices with their start and end apart: 3, of which 3 were waited for; matrix products, arithmetic and copies ran while one was open for 1% of the time, Pallas kernels for 0%

commit v1 on v0

v1 whole, which is shorter than its diff:
```python
import functools
import math

import jax
import jax.numpy as jnp
from jax import lax
from jax.experimental import pallas as pl
from jax.experimental.pallas import tpu as pltpu
from jax.sharding import PartitionSpec as P

beta_first = 0.9
beta_second = 0.999
epsilon = 1e-08
step_size = 0.25

F32 = jnp.float32
BF16 = jnp.bfloat16
MESH_ID = pl.DeviceIdType.MESH
OWN = 64
HALF = 16
DEPTH = 512


def halves(top, bottom, low):
    first = jnp.where(low, top, pltpu.roll(bottom, 64, 1))
    second = jnp.where(low, pltpu.roll(top, 64, 1), bottom)
    return first, second


def kernel(
    side, n_mp, act_hbm, cot_hbm, basis_hbm, weight_hbm, moment_hbm, second_hbm,
    weight_out, moment_out, second_out,
    act, cot, basis, weight, moment, second, new_weight, new_moment, new_second,
    partial, mp_send, mp_recv, rows_t, y_send, z_send, y_recv, z_recv,
    zz_send, yy_send, zz_recv, yy_recv, x_send, x_recv, gather,
    load_sem, part_sem, store_sem, mp_ss, mp_rs, y_ss, y_rs, z_ss, z_rs,
    zz_ss, zz_rs, yy_ss, yy_rs, x_ss, x_rs, g_ss, g_rs,
):
    dp = lax.axis_index("dp")
    mp = lax.axis_index("mp")
    y = lax.rem(dp, side)
    z = lax.rem(dp // side, side)
    x = dp // (side * side)

    def y_peer(k):
        return (dp - y + lax.rem(y + k, side), mp)

    def z_peer(k):
        return (dp + (lax.rem(z + k, side) - z) * side, mp)

    def mp_peer(k):
        return (dp, lax.rem(mp + k, n_mp))

    x_peer = (dp + (1 - 2 * x) * side * side, mp)

    def remote(src, dst, send_sem, recv_sem, device):
        return pltpu.make_async_remote_copy(
            src_ref=src, dst_ref=dst, send_sem=send_sem, recv_sem=recv_sem,
            device_id=device, device_id_type=MESH_ID,
        )

    tokens = act.shape[0]
    micro = tokens // 2
    depth_all = basis.shape[0]
    parts = depth_all // DEPTH

    def part_copies(i):
        span = pl.ds(i * DEPTH, DEPTH)
        return (
            pltpu.make_async_copy(basis_hbm.at[span, :], basis.at[span, :], part_sem.at[0, i]),
            pltpu.make_async_copy(cot_hbm.at[:, span], cot.at[:, span], part_sem.at[1, i]),
        )

    for i in range(parts):
        for copy in part_copies(i):
            copy.start()
    loads = [
        pltpu.make_async_copy(act_hbm, act, load_sem.at[0]),
        pltpu.make_async_copy(moment_hbm, moment, load_sem.at[1]),
        pltpu.make_async_copy(second_hbm, second, load_sem.at[2]),
        pltpu.make_async_copy(weight_hbm, weight, load_sem.at[3]),
    ]
    for copy in loads:
        copy.start()

    barrier = pltpu.get_barrier_semaphore()
    for k in range(1, n_mp):
        pl.semaphore_signal(barrier, inc=1, device_id=mp_peer(k), device_id_type=MESH_ID)
    for k in range(1, side):
        pl.semaphore_signal(barrier, inc=1, device_id=y_peer(k), device_id_type=MESH_ID)
        pl.semaphore_signal(barrier, inc=1, device_id=z_peer(k), device_id_type=MESH_ID)
    pl.semaphore_signal(barrier, inc=1, device_id=x_peer, device_id_type=MESH_ID)

    for i in range(parts):
        for copy in part_copies(i):
            copy.wait()
        span = slice(i * DEPTH, (i + 1) * DEPTH)
        term = jnp.dot(cot[:, span], basis[span, :], preferred_element_type=F32)
        if i == 0:
            partial[...] = term
        else:
            partial[...] += term

    low_micro = lax.broadcasted_iota(jnp.int32, (micro, 128), 1) < 64
    for t in range(n_mp // 2):
        cols = slice(t * 128, (t + 1) * 128)
        first, second_tile = halves(partial[:micro, cols], partial[micro:, cols], low_micro)
        mp_send[2 * t] = first.astype(BF16)
        mp_send[2 * t + 1] = second_tile.astype(BF16)

    pl.semaphore_wait(barrier, n_mp - 1 + 2 * (side - 1) + 1)

    def mp_copy(k):
        return remote(
            mp_send.at[lax.rem(mp + k, n_mp)], mp_recv.at[k - 1], mp_ss.at[k - 1], mp_rs.at[k - 1], mp_peer(k)
        )

    for k in range(1, n_mp):
        mp_copy(k).start()
    total = mp_send[mp].astype(F32)
    for k in range(1, n_mp):
        mp_copy(k).wait_recv()
        total = total + mp_recv[k - 1].astype(F32)
    projected = total.astype(BF16).astype(F32)
    stacked = jnp.concatenate(
        [projected, pltpu.roll(projected, 64, 1), jnp.zeros((256 - tokens, 128), F32)], axis=0
    )
    rows_t[...] = stacked.T[:OWN, :].astype(BF16)

    loads[0].wait()
    lhs = rows_t[:, :tokens]
    low = lax.broadcasted_iota(jnp.int32, (32, 128), 1) < 64

    def z_copy(k):
        return remote(
            z_send.at[lax.rem(z + k, side)], z_recv.at[k - 1], z_ss.at[k - 1], z_rs.at[k - 1], z_peer(k)
        )

    def y_copy(k):
        return remote(
            y_send.at[lax.rem(y + k, side)], y_recv.at[k - 1], y_ss.at[k - 1], y_rs.at[k - 1], y_peer(k)
        )

    width = side * OWN

    def gradient_of(k, carry):
        to_z = lax.rem(z + k, side)
        for to_x in range(2):
            start = pl.multiple_of((to_x * side + to_z) * width, 128)
            grad = jnp.dot(lhs, act[:, pl.ds(start, width)], preferred_element_type=F32)
            for pair in range(side // 2):
                tile = grad[:, pair * 128 : (pair + 1) * 128]
                for lo, block in enumerate(halves(tile[:32], tile[32:], low)):
                    block = block.astype(BF16)
                    y_send[2 * pair + lo, to_x, to_z] = block[:HALF]
                    z_send[to_z, to_x, 2 * pair + lo] = block[HALF:]

        @pl.when(k < side)
        def _():
            z_copy(k).start()

        return carry

    lax.fori_loop(1, side + 1, gradient_of, 0)
    for k in range(1, side):
        y_copy(k).start()

    def add_first(copy, send, recv, own, out):
        for k in range(1, side):
            copy(k).wait_recv()

        def body(q, carry):
            for to_x in range(2):
                acc = send[own, to_x, q].astype(F32)
                for k in range(side - 1):
                    acc = acc + recv[k, to_x, q].astype(F32)
                out[q, to_x] = acc.astype(BF16)
            return carry

        lax.fori_loop(0, side, body, 0)

    def yy_copy(k):
        return remote(
            yy_send.at[lax.rem(y + k, side)], yy_recv.at[k - 1], yy_ss.at[k - 1], yy_rs.at[k - 1], y_peer(k)
        )

    def zz_copy(k):
        return remote(
            zz_send.at[lax.rem(z + k, side)], zz_recv.at[k - 1], zz_ss.at[k - 1], zz_rs.at[k - 1], z_peer(k)
        )

    add_first(z_copy, z_send, z_recv, z, yy_send)
    for k in range(1, side):
        yy_copy(k).start()
    add_first(y_copy, y_send, y_recv, y, zz_send)
    for k in range(1, side):
        zz_copy(k).start()

    def add_second(copy, send, recv, own, half):
        acc = [send[own, to_x].astype(F32) for to_x in range(2)]
        for k in range(1, side):
            copy(k).wait_recv()
            for to_x in range(2):
                acc[to_x] = acc[to_x] + recv[k - 1, to_x].astype(F32)
        for to_x in range(2):
            x_send[to_x, half * HALF : (half + 1) * HALF, :] = acc[to_x]

    add_second(yy_copy, yy_send, yy_recv, y, 1)
    add_second(zz_copy, zz_send, zz_recv, z, 0)
    x_copy = remote(x_send.at[1 - x], x_recv, x_ss, x_rs, x_peer)
    x_copy.start()
    x_copy.wait_recv()
    packed = x_send[x] + x_recv[...]
    grad_t = jnp.concatenate([packed, pltpu.roll(packed, 64, 1)], axis=0)
    grad = grad_t.T[:OWN, :]

    loads[1].wait()
    loads[2].wait()
    moment_new = beta_first * moment[...] + (1.0 - beta_first) * grad
    second_new = beta_second * second[...] + (1.0 - beta_second) * grad * grad
    new_moment[...] = moment_new
    new_second[...] = second_new
    direction = moment_new / (jnp.sqrt(second_new) + epsilon)
    twice = jnp.concatenate([direction, direction], axis=1)
    mine = lax.broadcasted_iota(jnp.int32, (OWN, 128), 1) // 64 == lax.rem(mp, 2)
    gather[mp] = jnp.where(mine, twice, 0.0).astype(BF16)

    def g_copy(k):
        return remote(gather.at[mp], gather.at[mp], g_ss.at[k - 1], g_rs.at[k - 1], mp_peer(k))

    def g_arrival(k):
        slot = lax.rem(mp + n_mp - k, n_mp)
        return remote(gather.at[slot], gather.at[slot], g_ss.at[k - 1], g_rs.at[k - 1], mp_peer(k))

    for k in range(1, n_mp):
        g_copy(k).start()
    stores = [
        pltpu.make_async_copy(new_moment, moment_out, store_sem.at[0]),
        pltpu.make_async_copy(new_second, second_out, store_sem.at[1]),
    ]
    for copy in stores:
        copy.start()
    loads[3].wait()
    for k in range(1, n_mp):
        g_arrival(k).wait_recv()
    left = jnp.concatenate([gather[2 * t] + gather[2 * t + 1] for t in range(n_mp // 2)], axis=1)

    for i in range(parts):
        span = slice(i * DEPTH, (i + 1) * DEPTH)
        update = lax.dot_general(left, basis[span, :], (((1,), (1,)), ((), ())), preferred_element_type=F32)
        new_weight[:, span] = (weight[:, span].astype(F32) - step_size * update).astype(BF16)
    stores.append(pltpu.make_async_copy(new_weight, weight_out, store_sem.at[2]))
    stores[-1].start()

    for k in range(1, n_mp):
        mp_copy(k).wait_send()
        g_copy(k).wait_send()
    for k in range(1, side):
        z_copy(k).wait_send()
        y_copy(k).wait_send()
        yy_copy(k).wait_send()
        zz_copy(k).wait_send()
    x_copy.wait_send()
    for copy in stores:
        copy.wait()


def shards(side, n_mp, activations, cotangent, subspace_basis, weight, moment, second):
    micro, tokens, width = activations.shape
    act = activations.reshape(micro * tokens, width)
    cot = cotangent.reshape(micro * tokens, cotangent.shape[2])
    units, rank = subspace_basis.shape
    dma = pltpu.SemaphoreType.DMA
    n = side - 1
    m = n_mp - 1
    block = (2, HALF, 128)
    plane = (2, side, HALF, 128)
    scratch = [
        pltpu.VMEM(act.shape, BF16),
        pltpu.VMEM(cot.shape, BF16),
        pltpu.VMEM(subspace_basis.shape, BF16),
        pltpu.VMEM(weight.shape, BF16),
        pltpu.VMEM(moment.shape, F32),
        pltpu.VMEM(second.shape, F32),
        pltpu.VMEM(weight.shape, BF16),
        pltpu.VMEM(moment.shape, F32),
        pltpu.VMEM(second.shape, F32),
        pltpu.VMEM((micro * tokens, rank), F32),
        pltpu.VMEM((n_mp, tokens, 128), BF16),
        pltpu.VMEM((m, tokens, 128), BF16),
        pltpu.VMEM((OWN, 256), BF16),
        pltpu.VMEM((side,) + plane, BF16),
        pltpu.VMEM((side,) + plane, BF16),
        pltpu.VMEM((n,) + plane, BF16),
        pltpu.VMEM((n,) + plane, BF16),
        pltpu.VMEM((side,) + block, BF16),
        pltpu.VMEM((side,) + block, BF16),
        pltpu.VMEM((n,) + block, BF16),
        pltpu.VMEM((n,) + block, BF16),
        pltpu.VMEM((2, 32, 128), F32),
        pltpu.VMEM((32, 128), F32),
        pltpu.VMEM((n_mp, OWN, 128), BF16),
        dma((4,)),
        dma((2, units // DEPTH)),
        dma((3,)),
        dma((m,)), dma((m,)),
        dma((n,)), dma((n,)), dma((n,)), dma((n,)),
        dma((n,)), dma((n,)), dma((n,)), dma((n,)),
        dma(()), dma(()),
        dma((m,)), dma((m,)),
    ]
    hbm = pl.BlockSpec(memory_space=pltpu.HBM)
    rows, owned_units = weight.shape
    return pl.pallas_call(
        functools.partial(kernel, side, n_mp),
        out_shape=(
            jax.ShapeDtypeStruct(weight.shape, BF16),
            jax.ShapeDtypeStruct(moment.shape, F32),
            jax.ShapeDtypeStruct(second.shape, F32),
        ),
        in_specs=[hbm] * 6,
        out_specs=(hbm,) * 3,
        scratch_shapes=scratch,
        compiler_params=pltpu.CompilerParams(
            collective_id=0, has_side_effects=True, vmem_limit_bytes=60 * 1024 * 1024
        ),
    )(act, cot, subspace_basis, weight, moment, second)


def solution(mesh):
    side = math.isqrt(mesh.shape["dp"] // 2)
    n_mp = mesh.shape["mp"]
    in_specs = (
        P(None, "dp", None),
        P(None, "dp", "mp"),
        P("mp", None),
        P("dp", "mp"),
        P("dp", "mp"),
        P("dp", "mp"),
    )
    out_specs = (P("dp", "mp"), P("dp", "mp"), P("dp", "mp"))
    return jax.shard_map(
        functools.partial(shards, side, n_mp), mesh=mesh, in_specs=in_specs, out_specs=out_specs, check_vma=False
    )
```

time: 776 us -> 69.4 us (0.09)
  waiting for transfers between devices: 620 us -> 0 us
  blocking collectives: 118 us -> 0 us
  Pallas kernels: 0 us -> 63.9 us
  matrix products: 18 us -> 0 us
  between operations: 13.8 us -> 0.64 us
    unnamed x4 -> x0, waiting for transfers between devices: 529 us -> none
    all_gather x1 -> x0, blocking collectives: 118 us -> none  [shards(): lax.all_gather(direction, 'mp', axis=1, tiled=True)]
    reduce_scatter x2 -> x0, waiting for transfers between devices: 91.4 us -> none  [shards(): lax.psum_scatter(lax.dot_general(subspace_basis, cotangent[number], (((0,...]
    pallas_call x0 -> x1, Pallas kernels: none -> 63.9 us  [shards(): pl.pallas_call(functools.partial(kernel, side, n_mp), out_shape=(jax.Shap...]
    dot_general x5 -> x0, matrix products: 18 us -> none  [the longest x2 8.1 us: shards(): lax.dot_general(subspace_basis, cotangent[number], (((0,), (1,)), ((), ()...]
  transfers between devices with their start and end apart: 3 -> 0, of which waited for: 3 -> 0; matrix products, arithmetic and copies ran while one was open for 1% -> 0% of each run, Pallas kernels for 0% -> 0%
where the time goes in v1:
time: 69.4 us; the launch traced here: 69.1 us
  Pallas kernels  63.9 us (92%)
  local copies, waits for them, and re-layouts  4.56 us (7%)
    pallas_call x1, Pallas kernels, shards(): pl.pallas_call(functools.partial(kernel, side, n_mp), out_shape=(jax.Shap...  63.9 us
    unnamed x3, local copies, waits for them, and re-layouts  4.56 us

profile of v1, /device:TPU:1, one launch (start us, length us, event | category | flops | bytes accessed | tf_op | source)
XLA Modules:
  0.0 69.1 jit_solution(12431183970262818989)
XLA Ops:
  0.6 63.9 %shard_map.85 = (bf16[64,3584]{1,0:T(8,128)(2,1)}, f32[64,64]{1,0:T(8,128)}, f32[64,64]{1,0:T(8,128)}) custom-call(bf16[224,8192]{1,0:T(8,128)(2,1)} %bitcast.2, bf16[224,3584]{1,0:T(8,128)(2,1)} %bitcast.3, bf16[3584,512]{1,0:T(8,128)(2,1)} %basis_hbm.1, bf16[64,3584]{1,0:T(8,128)(2,1)} %weight_hbm.1, f32[64,64]{1,0:T(8,128)} %moment_hbm.1, f32[64,64]{1,0:T(8,128)} %second_hbm.1), custom_call_target="tpu_custom_call" | custom-call | tf_op jit(solution)/shard_map/pallas_call | solution.py:314
  64.5 1.8 %copy.12 = bf16[64,3584]{1,0:T(8,128)(2,1)} copy(bf16[64,3584]{1,0:T(8,128)(2,1)} %get-tuple-element.6) | data formatting | bytes 917504
  66.3 1.4 %copy.13 = f32[64,64]{1,0:T(8,128)} copy(f32[64,64]{1,0:T(8,128)} %get-tuple-element.7) | data formatting | bytes 32768
  67.7 1.4 %copy.14 = f32[64,64]{1,0:T(8,128)} copy(f32[64,64]{1,0:T(8,128)} %get-tuple-element.8) | data formatting | bytes 32768

commit v2 on v1

v2 whole, which is shorter than its diff:
```python
import functools
import math

import jax
import jax.numpy as jnp
from jax import lax
from jax.experimental import pallas as pl
from jax.experimental.pallas import tpu as pltpu
from jax.sharding import PartitionSpec as P

beta_first = 0.9
beta_second = 0.999
epsilon = 1e-08
step_size = 0.25

F32 = jnp.float32
BF16 = jnp.bfloat16
MESH_ID = pl.DeviceIdType.MESH
OWN = 64
HALF = 16
DEPTH = 512


def halves(top, bottom, low):
    first = jnp.where(low, top, pltpu.roll(bottom, 64, 1))
    second = jnp.where(low, pltpu.roll(top, 64, 1), bottom)
    return first, second


def low_lanes(rows):
    return lax.broadcasted_iota(jnp.int32, (rows, 128), 1) < 64


def gradient_kernel(
    side, n_mp, act_hbm, cot_hbm, basis_hbm, moment_hbm, second_hbm,
    gather_out, grad_out,
    act, cot, basis, moment, second, grad_own,
    partial, mp_send, mp_recv, rows_t, y_send, z_send,
    y_recv1, y_recv2, y_recv3, y_recv4, z_recv1, z_recv2, z_recv3, z_recv4,
    zz_send, yy_send, zz_recv, yy_recv, x_send, x_recv, gather,
    load_sem, part_sem, store_sem, mp_ss, mp_rs, y_ss, y_rs, z_ss, z_rs,
    zz_ss, zz_rs, yy_ss, yy_rs, x_ss, x_rs, g_ss, g_rs,
):
    dp = lax.axis_index("dp")
    mp = lax.axis_index("mp")
    y = lax.rem(dp, side)
    z = lax.rem(dp // side, side)
    x = dp // (side * side)

    def y_peer(k):
        return (dp - y + lax.rem(y + k, side), mp)

    def z_peer(k):
        return (dp + (lax.rem(z + k, side) - z) * side, mp)

    def mp_peer(k):
        return (dp, lax.rem(mp + k, n_mp))

    x_peer = (dp + (1 - 2 * x) * side * side, mp)

    def remote(src, dst, send_sem, recv_sem, device):
        return pltpu.make_async_remote_copy(
            src_ref=src, dst_ref=dst, send_sem=send_sem, recv_sem=recv_sem,
            device_id=device, device_id_type=MESH_ID,
        )

    tokens = act.shape[0]
    micro = tokens // 2
    parts = basis.shape[0] // DEPTH

    def part_copies(i):
        span = pl.ds(i * DEPTH, DEPTH)
        return (
            pltpu.make_async_copy(basis_hbm.at[span, :], basis.at[span, :], part_sem.at[0, i]),
            pltpu.make_async_copy(cot_hbm.at[:, span], cot.at[:, span], part_sem.at[1, i]),
        )

    for i in range(parts):
        for copy in part_copies(i):
            copy.start()
    loads = [
        pltpu.make_async_copy(act_hbm, act, load_sem.at[0]),
        pltpu.make_async_copy(moment_hbm, moment, load_sem.at[1]),
        pltpu.make_async_copy(second_hbm, second, load_sem.at[2]),
    ]
    for copy in loads:
        copy.start()

    barrier = pltpu.get_barrier_semaphore()
    for k in range(1, n_mp):
        pl.semaphore_signal(barrier, inc=1, device_id=mp_peer(k), device_id_type=MESH_ID)
    for k in range(1, side):
        pl.semaphore_signal(barrier, inc=1, device_id=y_peer(k), device_id_type=MESH_ID)
        pl.semaphore_signal(barrier, inc=1, device_id=z_peer(k), device_id_type=MESH_ID)
    pl.semaphore_signal(barrier, inc=1, device_id=x_peer, device_id_type=MESH_ID)

    for i in range(parts):
        for copy in part_copies(i):
            copy.wait()
        span = slice(i * DEPTH, (i + 1) * DEPTH)
        term = jnp.dot(cot[:, span], basis[span, :], preferred_element_type=F32)
        if i == 0:
            partial[...] = term
        else:
            partial[...] += term

    for t in range(n_mp // 2):
        cols = slice(t * 128, (t + 1) * 128)
        first, other = halves(partial[:micro, cols], partial[micro:, cols], low_lanes(micro))
        mp_send[2 * t] = first.astype(BF16)
        mp_send[2 * t + 1] = other.astype(BF16)

    pl.semaphore_wait(barrier, n_mp - 1 + 2 * (side - 1) + 1)

    def mp_copy(k):
        return remote(
            mp_send.at[lax.rem(mp + k, n_mp)], mp_recv.at[k - 1], mp_ss.at[k - 1], mp_rs.at[k - 1], mp_peer(k)
        )

    for k in range(1, n_mp):
        mp_copy(k).start()
    total = mp_send[mp].astype(F32)
    for k in range(1, n_mp):
        mp_copy(k).wait_recv()
        total = total + mp_recv[k - 1].astype(F32)
    projected = total.astype(BF16).astype(F32)
    stacked = jnp.concatenate(
        [projected, pltpu.roll(projected, 64, 1), jnp.zeros((256 - tokens, 128), F32)], axis=0
    )
    rows_t[...] = stacked.T[:OWN, :].astype(BF16)

    loads[0].wait()
    y_lhs = rows_t[:32, :tokens]
    z_lhs = rows_t[32:, :tokens]
    width = side * OWN

    def z_blocks(offset):
        to_z = lax.rem(z + offset, side)
        for to_x in range(2):
            start = pl.multiple_of((to_x * side + to_z) * width, 128)
            grad = jnp.dot(z_lhs, act[:, pl.ds(start, width)], preferred_element_type=F32)
            for pair in range(side // 2):
                tile = grad[:, pair * 128 : (pair + 1) * 128]
                for lo, block in enumerate(halves(tile[:HALF], tile[HALF:], low_lanes(HALF))):
                    z_send[to_z, to_x, 2 * pair + lo] = block.astype(BF16)

    def y_blocks(offset):
        pair = lax.rem(y // 2 + offset, side // 2)
        for to_x in range(2):
            for q in range(side // 2):
                tiles = []
                for to_z in (2 * q, 2 * q + 1):
                    start = pl.multiple_of((to_x * side + to_z) * width + pair * 128, 128)
                    tiles.append(act[:, pl.ds(start, 128)])
                grad = jnp.dot(y_lhs, jnp.concatenate(tiles, axis=1), preferred_element_type=F32)
                for r in range(2):
                    tile = grad[:, r * 128 : (r + 1) * 128]
                    for lo, block in enumerate(halves(tile[:HALF], tile[HALF:], low_lanes(HALF))):
                        y_send[2 * pair + lo, to_x, 2 * q + r] = block.astype(BF16)

    def axis(pos, peer, send, recv1, recv2, recv3, recv4, ss, rs):
        def block(offset):
            return send.at[lax.rem(pos + offset, side)]

        up, down = (1, 2, 3), (side - 1, side - 2, side - 3)
        near, merged, far, across = [], [], [], []
        for way, (one, two, three) in enumerate((up, down)):
            near.append(remote(block(one), recv1.at[way], ss.at[0, way], rs.at[0, way], peer(one)))
            merged.append(remote(block(two), recv2.at[way], ss.at[1, way], rs.at[1, way], peer(two)))
            far.append(remote(block(three), recv3.at[way], ss.at[2, way], rs.at[2, way], peer(one)))
            across.append(remote(block(4).at[way], recv4.at[way], ss.at[3, way], rs.at[3, way], peer(two)))

        def merge():
            for way, two in enumerate((2, side - 2)):
                slot = lax.rem(pos + two, side)
                far[way].wait_recv()
                across[way].wait_recv()
                for to_x in range(2):
                    acc = send[slot, to_x].astype(F32) + recv3[way, to_x].astype(F32)
                    if to_x == way:
                        acc = acc + recv4[way].astype(F32)
                    send[slot, to_x] = acc.astype(BF16)
                merged[way].start()

        def total(out):
            for way in range(2):
                near[way].wait_recv()
                merged[way].wait_recv()
            for to_x in range(2):
                acc = send[pos, to_x].astype(F32)
                for recv in (recv1, recv2):
                    for way in range(2):
                        acc = acc + recv[way, to_x].astype(F32)
                acc = acc.astype(BF16)
                for q in range(side):
                    out[q, to_x] = acc[q]

        return near, merged, far, across, merge, total

    z_near, z_merged, z_far, z_across, z_merge, z_total = axis(
        z, z_peer, z_send, z_recv1, z_recv2, z_recv3, z_recv4, z_ss, z_rs
    )
    y_near, y_merged, y_far, y_across, y_merge, y_total = axis(
        y, y_peer, y_send, y_recv1, y_recv2, y_recv3, y_recv4, y_ss, y_rs
    )

    def begin(copies):
        for copy in copies:
            copy.start()

    z_blocks(4)
    begin(z_across)
    z_blocks(3)
    z_blocks(side - 3)
    begin(z_far)
    y_blocks(2)
    begin(y_across)
    y_blocks(1)
    y_blocks(3)
    begin(y_far)
    z_blocks(1)
    z_blocks(side - 1)
    begin(z_near)
    y_blocks(0)
    begin(y_near)
    z_blocks(2)
    z_blocks(side - 2)
    z_merge()
    y_merge()
    z_blocks(0)

    def yy_copy(k):
        return remote(
            yy_send.at[lax.rem(y + k, side)], yy_recv.at[k - 1], yy_ss.at[k - 1], yy_rs.at[k - 1], y_peer(k)
        )

    def zz_copy(k):
        return remote(
            zz_send.at[lax.rem(z + k, side)], zz_recv.at[k - 1], zz_ss.at[k - 1], zz_rs.at[k - 1], z_peer(k)
        )

    z_total(yy_send)
    for k in range(1, side):
        yy_copy(k).start()
    y_total(zz_send)
    for k in range(1, side):
        zz_copy(k).start()

    def add_second(copy, send, recv, own, half):
        acc = [send[own, to_x].astype(F32) for to_x in range(2)]
        for k in range(1, side):
            copy(k).wait_recv()
            for to_x in range(2):
                acc[to_x] = acc[to_x] + recv[k - 1, to_x].astype(F32)
        for to_x in range(2):
            x_send[to_x, half * HALF : (half + 1) * HALF, :] = acc[to_x]

    add_second(yy_copy, yy_send, yy_recv, y, 1)
    add_second(zz_copy, zz_send, zz_recv, z, 0)
    x_copy = remote(x_send.at[1 - x], x_recv, x_ss, x_rs, x_peer)
    x_copy.start()
    x_copy.wait_recv()
    packed = x_send[x] + x_recv[...]
    rolled = pltpu.roll(packed, 64, 1)
    grad_t = jnp.concatenate([packed[:HALF], rolled[:HALF], packed[HALF:], rolled[HALF:]], axis=0)
    grad = grad_t.T[:OWN, :]

    loads[1].wait()
    loads[2].wait()
    moment_new = beta_first * moment[...] + (1.0 - beta_first) * grad
    second_new = beta_second * second[...] + (1.0 - beta_second) * grad * grad
    direction = moment_new / (jnp.sqrt(second_new) + epsilon)
    gather[mp] = jnp.concatenate([direction[:32], direction[32:]], axis=1).astype(BF16)

    def g_copy(k):
        return remote(gather.at[mp], gather.at[mp], g_ss.at[k - 1], g_rs.at[k - 1], mp_peer(k))

    def g_arrival(k):
        slot = lax.rem(mp + n_mp - k, n_mp)
        return remote(gather.at[slot], gather.at[slot], g_ss.at[k - 1], g_rs.at[k - 1], mp_peer(k))

    for k in range(1, n_mp):
        g_copy(k).start()
    grad_own[...] = grad
    grad_store = pltpu.make_async_copy(grad_own, grad_out, store_sem.at[0])
    grad_store.start()
    for k in range(1, n_mp):
        mp_copy(k).wait_send()
    for copies in (z_near, z_merged, z_far, z_across, y_near, y_merged, y_far, y_across):
        for copy in copies:
            copy.wait_send()
    for k in range(1, side):
        yy_copy(k).wait_send()
        zz_copy(k).wait_send()
    x_copy.wait_send()
    for k in range(1, n_mp):
        g_arrival(k).wait_recv()
    gather_store = pltpu.make_async_copy(gather, gather_out, store_sem.at[1])
    gather_store.start()
    for k in range(1, n_mp):
        g_copy(k).wait_send()
    grad_store.wait()
    gather_store.wait()


def weight_kernel(
    n_mp, gather_hbm, grad_hbm, basis_hbm, weight_hbm, moment_hbm, second_hbm,
    weight_out, moment_out, second_out,
    gather, grad, basis, weight, moment, second, new_weight, new_moment, new_second, load_sem, part_sem, store_sem,
):
    parts = basis.shape[0] // DEPTH

    def part_copy(i):
        span = pl.ds(i * DEPTH, DEPTH)
        return pltpu.make_async_copy(basis_hbm.at[span, :], basis.at[span, :], part_sem.at[0, i])

    def out_copy(i):
        span = pl.ds(i * DEPTH, DEPTH)
        return pltpu.make_async_copy(new_weight.at[:, span], weight_out.at[:, span], part_sem.at[1, i])

    loads = [
        pltpu.make_async_copy(source, target, load_sem.at[i])
        for i, (source, target) in enumerate(
            ((gather_hbm, gather), (weight_hbm, weight), (grad_hbm, grad), (moment_hbm, moment), (second_hbm, second))
        )
    ]
    loads[0].start()
    part_copy(0).start()
    loads[1].start()
    for i in range(1, parts):
        part_copy(i).start()
    for copy in loads[2:]:
        copy.start()
    loads[0].wait()
    tiles = []
    for t in range(n_mp // 2):
        top, bottom = halves(gather[2 * t].astype(F32), gather[2 * t + 1].astype(F32), low_lanes(32))
        tiles.append(jnp.concatenate([top, bottom], axis=0).astype(BF16))
    left = jnp.concatenate(tiles, axis=1)
    loads[1].wait()
    for i in range(parts):
        part_copy(i).wait()
        span = slice(i * DEPTH, (i + 1) * DEPTH)
        update = lax.dot_general(left, basis[span, :], (((1,), (1,)), ((), ())), preferred_element_type=F32)
        new_weight[:, span] = (weight[:, span].astype(F32) - step_size * update).astype(BF16)
        out_copy(i).start()
    for copy in loads[2:]:
        copy.wait()
    new_moment[...] = beta_first * moment[...] + (1.0 - beta_first) * grad[...]
    new_second[...] = beta_second * second[...] + (1.0 - beta_second) * grad[...] * grad[...]
    stores = [
        pltpu.make_async_copy(new_moment, moment_out, store_sem.at[0]),
        pltpu.make_async_copy(new_second, second_out, store_sem.at[1]),
    ]
    for copy in stores:
        copy.start()
    for i in range(parts):
        out_copy(i).wait()
    for copy in stores:
        copy.wait()


def shards(side, n_mp, activations, cotangent, subspace_basis, weight, moment, second):
    micro, tokens, width = activations.shape
    act = activations.reshape(micro * tokens, width)
    cot = cotangent.reshape(micro * tokens, cotangent.shape[2])
    units, rank = subspace_basis.shape
    dma = pltpu.SemaphoreType.DMA
    n = side - 1
    m = n_mp - 1
    block = (2, HALF, 128)
    plane = (side, HALF, 128)
    axis_recv = [
        pltpu.VMEM((2, 2) + plane, BF16),
        pltpu.VMEM((2, 2) + plane, BF16),
        pltpu.VMEM((2, 2) + plane, BF16),
        pltpu.VMEM((2,) + plane, BF16),
    ]
    scratch = [
        pltpu.VMEM(act.shape, BF16),
        pltpu.VMEM(cot.shape, BF16),
        pltpu.VMEM(subspace_basis.shape, BF16),
        pltpu.VMEM(moment.shape, F32),
        pltpu.VMEM(second.shape, F32),
        pltpu.VMEM(moment.shape, F32),
        pltpu.VMEM((micro * tokens, rank), F32),
        pltpu.VMEM((n_mp, tokens, 128), BF16),
        pltpu.VMEM((m, tokens, 128), BF16),
        pltpu.VMEM((OWN, 256), BF16),
        pltpu.VMEM((side, 2) + plane, BF16),
        pltpu.VMEM((side, 2) + plane, BF16),
        *axis_recv,
        *axis_recv,
        pltpu.VMEM((side,) + block, BF16),
        pltpu.VMEM((side,) + block, BF16),
        pltpu.VMEM((n,) + block, BF16),
        pltpu.VMEM((n,) + block, BF16),
        pltpu.VMEM((2, 32, 128), F32),
        pltpu.VMEM((32, 128), F32),
        pltpu.VMEM((n_mp, 32, 128), BF16),
        dma((3,)),
        dma((2, units // DEPTH)),
        dma((2,)),
        dma((m,)), dma((m,)),
        dma((4, 2)), dma((4, 2)), dma((4, 2)), dma((4, 2)),
        dma((n,)), dma((n,)), dma((n,)), dma((n,)),
        dma(()), dma(()),
        dma((m,)), dma((m,)),
    ]
    hbm = pl.BlockSpec(memory_space=pltpu.HBM)
    gathered, grad = pl.pallas_call(
        functools.partial(gradient_kernel, side, n_mp),
        out_shape=(
            jax.ShapeDtypeStruct((n_mp, 32, 128), BF16),
            jax.ShapeDtypeStruct(moment.shape, F32),
        ),
        in_specs=[hbm] * 5,
        out_specs=(hbm,) * 2,
        scratch_shapes=scratch,
        compiler_params=pltpu.CompilerParams(
            collective_id=0, has_side_effects=True, vmem_limit_bytes=60 * 1024 * 1024
        ),
    )(act, cot, subspace_basis, moment, second)
    return pl.pallas_call(
        functools.partial(weight_kernel, n_mp),
        out_shape=(
            jax.ShapeDtypeStruct(weight.shape, BF16),
            jax.ShapeDtypeStruct(moment.shape, F32),
            jax.ShapeDtypeStruct(second.shape, F32),
        ),
        in_specs=[hbm] * 6,
        out_specs=(hbm,) * 3,
        scratch_shapes=[
            pltpu.VMEM((n_mp, 32, 128), BF16),
            pltpu.VMEM(moment.shape, F32),
            pltpu.VMEM(subspace_basis.shape, BF16),
            pltpu.VMEM(weight.shape, BF16),
            pltpu.VMEM(moment.shape, F32),
            pltpu.VMEM(second.shape, F32),
            pltpu.VMEM(weight.shape, BF16),
            pltpu.VMEM(moment.shape, F32),
            pltpu.VMEM(second.shape, F32),
            dma((5,)),
            dma((2, units // DEPTH)),
            dma((2,)),
        ],
        compiler_params=pltpu.CompilerParams(vmem_limit_bytes=60 * 1024 * 1024),
    )(gathered, grad, subspace_basis, weight, moment, second)


def solution(mesh):
    side = math.isqrt(mesh.shape["dp"] // 2)
    n_mp = mesh.shape["mp"]
    in_specs = (
        P(None, "dp", None),
        P(None, "dp", "mp"),
        P("mp", None),
        P("dp", "mp"),
        P("dp", "mp"),
        P("dp", "mp"),
    )
    out_specs = (P("dp", "mp"), P("dp", "mp"), P("dp", "mp"))
    return jax.shard_map(
        functools.partial(shards, side, n_mp), mesh=mesh, in_specs=in_specs, out_specs=out_specs, check_vma=False
    )
```

time: 69.4 us -> 61.2 us (0.88)
  local copies, waits for them, and re-layouts: 4.56 us -> 0 us
  Pallas kernels: 63.9 us -> 60.4 us
    unnamed x3 -> x0, local copies, waits for them, and re-layouts: 4.56 us -> none
    pallas_call x1 -> x2, Pallas kernels: 63.9 us -> 60.4 us  [the longest x1 56.1 us: shards(): pl.pallas_call(functools.partial(gradient_kernel, side, n_mp), out_shape=...]
where the time goes in v2:
time: 61.2 us; the launch traced here: 61 us
  Pallas kernels  60.4 us (99%)
  between operations  0.64 us (1%)
    pallas_call x1, Pallas kernels, shards(): pl.pallas_call(functools.partial(gradient_kernel, side, n_mp), out_shape=...  56.1 us
    pallas_call x1, Pallas kernels, shards(): pl.pallas_call(functools.partial(weight_kernel, n_mp), out_shape=(jax.Sha...  4.35 us

profile of v2, /device:TPU:1, one launch (start us, length us, event | category | flops | bytes accessed | tf_op | source)
XLA Modules:
  0.0 61.0 jit_solution(8734789390601828209)
XLA Ops:
  0.6 56.1 %shard_map.85 = (bf16[8,32,128]{2,1,0:T(8,128)(2,1)}, f32[64,64]{1,0:T(8,128)}) custom-call(bf16[224,8192]{1,0:T(8,128)(2,1)} %bitcast.2, bf16[224,3584]{1,0:T(8,128)(2,1)} %bitcast.3, bf16[3584,512]{1,0:T(8,128)(2,1)} %basis_hbm.3, f32[64,64]{1,0:T(8,128)} %moment_hbm.3, f32[64,64]{1,0:T(8,128)} %second_hbm.3), custom_call_target="tpu_custom_call" | custom-call | tf_op jit(solution)/shard_map/pallas_call | solution.py:411
  56.7 4.4 %shard_map.86 = (bf16[64,3584]{1,0:T(8,128)(2,1)}, f32[64,64]{1,0:T(8,128)}, f32[64,64]{1,0:T(8,128)}) custom-call(bf16[8,32,128]{2,1,0:T(8,128)(2,1)} %get-tuple-element.5.gather_hbm, f32[64,64]{1,0:T(8,128)} %get-tuple-element.6.grad_hbm, bf16[3584,512]{1,0:T(8,128)(2,1)} %basis_hbm.3, bf16[64,3584]{1,0:T(8,128)(2,1)} %weight_hbm.1, f32[64,64]{1,0:T(8,128)} %moment_hbm.3, ...), custom_call_target="tpu_custom_call" | custom-call | tf_op jit(solution)/shard_map/pallas_call | solution.py:424

commit v3 on v2

--- a/solution.py
+++ b/solution.py
@@ -19,6 +19,7 @@
 OWN = 64
 HALF = 16
 DEPTH = 512
+VMEM = 60 * 1024 * 1024
 
 
 def halves(top, bottom, low):
@@ -27,19 +28,23 @@
     return first, second
 
 
+def far_first(n):
+    return sorted(range(1, n), key=lambda k: (-min(k, n - k), k))
+
+
 def low_lanes(rows):
     return lax.broadcasted_iota(jnp.int32, (rows, 128), 1) < 64
 
 
-def gradient_kernel(
-    side, n_mp, act_hbm, cot_hbm, basis_hbm, moment_hbm, second_hbm,
-    gather_out, grad_out,
-    act, cot, basis, moment, second, grad_own,
+def step_kernel(
+    side, n_mp, act_hbm, cot_hbm, basis_hbm, weight_hbm, moment_hbm, second_hbm,
+    weight_out, moment_out, second_out,
+    act, cot, basis, weight, moment, second, new_weight, new_moment, new_second,
     partial, mp_send, mp_recv, rows_t, y_send, z_send,
     y_recv1, y_recv2, y_recv3, y_recv4, z_recv1, z_recv2, z_recv3, z_recv4,
-    zz_send, yy_send, zz_recv, yy_recv, x_send, x_recv, gather,
+    zz_send, yy_send, zz_recv, yy_recv, gather,
     load_sem, part_sem, store_sem, mp_ss, mp_rs, y_ss, y_rs, z_ss, z_rs,
-    zz_ss, zz_rs, yy_ss, yy_rs, x_ss, x_rs, g_ss, g_rs,
+    zz_ss, zz_rs, yy_ss, yy_rs, g_ss, g_rs,
 ):
     dp = lax.axis_index("dp")
     mp = lax.axis_index("mp")
@@ -56,7 +61,11 @@
     def mp_peer(k):
         return (dp, lax.rem(mp + k, n_mp))
 
-    x_peer = (dp + (1 - 2 * x) * side * side, mp)
+    def xy_peer(k, flip):
+        return (dp + flip * (1 - 2 * x) * side * side - y + lax.rem(y + k, side), mp)
+
+    def xz_peer(k, flip):
+        return (dp + flip * (1 - 2 * x) * side * side + (lax.rem(z + k, side) - z) * side, mp)
 
     def remote(src, dst, send_sem, recv_sem, device):
         return pltpu.make_async_remote_copy(
@@ -82,6 +91,7 @@
         pltpu.make_async_copy(act_hbm, act, load_sem.at[0]),
         pltpu.make_async_copy(moment_hbm, moment, load_sem.at[1]),
         pltpu.make_async_copy(second_hbm, second, load_sem.at[2]),
+        pltpu.make_async_copy(weight_hbm, weight, load_sem.at[3]),
     ]
     for copy in loads:
         copy.start()
@@ -89,10 +99,11 @@
     barrier = pltpu.get_barrier_semaphore()
     for k in range(1, n_mp):
         pl.semaphore_signal(barrier, inc=1, device_id=mp_peer(k), device_id_type=MESH_ID)
-    for k in range(1, side):
-        pl.semaphore_signal(barrier, inc=1, device_id=y_peer(k), device_id_type=MESH_ID)
-        pl.semaphore_signal(barrier, inc=1, device_id=z_peer(k), device_id_type=MESH_ID)
-    pl.semaphore_signal(barrier, inc=1, device_id=x_peer, device_id_type=MESH_ID)
+    for flip in range(2):
+        for k in range(1, side):
+            pl.semaphore_signal(barrier, inc=1, device_id=xy_peer(k, flip), device_id_type=MESH_ID)
+            pl.semaphore_signal(barrier, inc=1, device_id=xz_peer(k, flip), device_id_type=MESH_ID)
+    pl.semaphore_signal(barrier, inc=1, device_id=xy_peer(0, 1), device_id_type=MESH_ID)
 
     for i in range(parts):
         for copy in part_copies(i):
@@ -110,17 +121,17 @@
         mp_send[2 * t] = first.astype(BF16)
         mp_send[2 * t + 1] = other.astype(BF16)
 
-    pl.semaphore_wait(barrier, n_mp - 1 + 2 * (side - 1) + 1)
+    pl.semaphore_wait(barrier, n_mp - 1 + 4 * (side - 1) + 1)
 
     def mp_copy(k):
         return remote(
             mp_send.at[lax.rem(mp + k, n_mp)], mp_recv.at[k - 1], mp_ss.at[k - 1], mp_rs.at[k - 1], mp_peer(k)
         )
 
-    for k in range(1, n_mp):
+    for k in far_first(n_mp):
         mp_copy(k).start()
     total = mp_send[mp].astype(F32)
-    for k in range(1, n_mp):
+    for k in reversed(far_first(n_mp)):
         mp_copy(k).wait_recv()
         total = total + mp_recv[k - 1].astype(F32)
     projected = total.astype(BF16).astype(F32)
@@ -229,46 +240,42 @@
     y_merge()
     z_blocks(0)
 
-    def yy_copy(k):
-        return remote(
-            yy_send.at[lax.rem(y + k, side)], yy_recv.at[k - 1], yy_ss.at[k - 1], yy_rs.at[k - 1], y_peer(k)
-        )
-
-    def zz_copy(k):
-        return remote(
-            zz_send.at[lax.rem(z + k, side)], zz_recv.at[k - 1], zz_ss.at[k - 1], zz_rs.at[k - 1], z_peer(k)
-        )
-
+    targets = [(k, flip) for k in far_first(side) for flip in (1, 0)] + [(0, 1)]
+
+    def second_copies(pos, peer, send, recv, ss, rs):
+        return [
+            remote(
+                send.at[lax.rem(pos + k, side), x + flip * (1 - 2 * x)],
+                recv.at[i], ss.at[i], rs.at[i], peer(k, flip),
+            )
+            for i, (k, flip) in enumerate(targets)
+        ]
+
+    yy_copies = second_copies(y, xy_peer, yy_send, yy_recv, yy_ss, yy_rs)
+    zz_copies = second_copies(z, xz_peer, zz_send, zz_recv, zz_ss, zz_rs)
     z_total(yy_send)
-    for k in range(1, side):
-        yy_copy(k).start()
+    begin(yy_copies)
     y_total(zz_send)
-    for k in range(1, side):
-        zz_copy(k).start()
-
-    def add_second(copy, send, recv, own, half):
-        acc = [send[own, to_x].astype(F32) for to_x in range(2)]
-        for k in range(1, side):
-            copy(k).wait_recv()
-            for to_x in range(2):
-                acc[to_x] = acc[to_x] + recv[k - 1, to_x].astype(F32)
-        for to_x in range(2):
-            x_send[to_x, half * HALF : (half + 1) * HALF, :] = acc[to_x]
-
-    add_second(yy_copy, yy_send, yy_recv, y, 1)
-    add_second(zz_copy, zz_send, zz_recv, z, 0)
-    x_copy = remote(x_send.at[1 - x], x_recv, x_ss, x_rs, x_peer)
-    x_copy.start()
-    x_copy.wait_recv()
-    packed = x_send[x] + x_recv[...]
-    rolled = pltpu.roll(packed, 64, 1)
-    grad_t = jnp.concatenate([packed[:HALF], rolled[:HALF], packed[HALF:], rolled[HALF:]], axis=0)
+    begin(zz_copies)
+
+    def add_second(copies, send, recv, own):
+        acc = send[own, x].astype(F32)
+        for i in reversed(range(len(copies))):
+            copies[i].wait_recv()
+            acc = acc + recv[i].astype(F32)
+        return acc
+
+    z_half = add_second(yy_copies, yy_send, yy_recv, y)
+    y_half = add_second(zz_copies, zz_send, zz_recv, z)
+    grad_t = jnp.concatenate([y_half, pltpu.roll(y_half, 64, 1), z_half, pltpu.roll(z_half, 64, 1)], axis=0)
     grad = grad_t.T[:OWN, :]
 
     loads[1].wait()
     loads[2].wait()
     moment_new = beta_first * moment[...] + (1.0 - beta_first) * grad
     second_new = beta_second * second[...] + (1.0 - beta_second) * grad * grad
+    new_moment[...] = moment_new
+    new_second[...] = second_new
     direction = moment_new / (jnp.sqrt(second_new) + epsilon)
     gather[mp] = jnp.concatenate([direction[:32], direction[32:]], axis=1).astype(BF16)
 
@@ -279,84 +286,44 @@
         slot = lax.rem(mp + n_mp - k, n_mp)
         return remote(gather.at[slot], gather.at[slot], g_ss.at[k - 1], g_rs.at[k - 1], mp_peer(k))
 
-    for k in range(1, n_mp):
+    for k in far_first(n_mp):
         g_copy(k).start()
-    grad_own[...] = grad
-    grad_store = pltpu.make_async_copy(grad_own, grad_out, store_sem.at[0])
-    grad_store.start()
+    stores = [
+        pltpu.make_async_copy(new_moment, moment_out, store_sem.at[0]),
+        pltpu.make_async_copy(new_second, second_out, store_sem.at[1]),
+    ]
+    begin(stores)
     for k in range(1, n_mp):
         mp_copy(k).wait_send()
-    for copies in (z_near, z_merged, z_far, z_across, y_near, y_merged, y_far, y_across):
+    for copies in (z_near, z_merged, z_far, z_across, y_near, y_merged, y_far, y_across, yy_copies, zz_copies):
         for copy in copies:
             copy.wait_send()
-    for k in range(1, side):
-        yy_copy(k).wait_send()
-        zz_copy(k).wait_send()
-    x_copy.wait_send()
-    for k in range(1, n_mp):
+    loads[3].wait()
+    for k in reversed(far_first(n_mp)):
         g_arrival(k).wait_recv()
-    gather_store = pltpu.make_async_copy(gather, gather_out, store_sem.at[1])
-    gather_store.start()
-    for k in range(1, n_mp):
-        g_copy(k).wait_send()
-    grad_store.wait()
-    gather_store.wait()
-
-
-def weight_kernel(
-    n_mp, gather_hbm, grad_hbm, basis_hbm, weight_hbm, moment_hbm, second_hbm,
-    weight_out, moment_out, second_out,
-    gather, grad, basis, weight, moment, second, new_weight, new_moment, new_second, load_sem, part_sem, store_sem,
-):
-    parts = basis.shape[0] // DEPTH
-
-    def part_copy(i):
-        span = pl.ds(i * DEPTH, DEPTH)
-        return pltpu.make_async_copy(basis_hbm.at[span, :], basis.at[span, :], part_sem.at[0, i])
-
-    def out_copy(i):
-        span = pl.ds(i * DEPTH, DEPTH)
-        return pltpu.make_async_copy(new_weight.at[:, span], weight_out.at[:, span], part_sem.at[1, i])
-
-    loads = [
-        pltpu.make_async_copy(source, target, load_sem.at[i])
-        for i, (source, target) in enumerate(
-            ((gather_hbm, gather), (weight_hbm, weight), (grad_hbm, grad), (moment_hbm, moment), (second_hbm, second))
-        )
-    ]
-    loads[0].start()
-    part_copy(0).start()
-    loads[1].start()
-    for i in range(1, parts):
-        part_copy(i).start()
-    for copy in loads[2:]:
-        copy.start()
-    loads[0].wait()
     tiles = []
     for t in range(n_mp // 2):
         top, bottom = halves(gather[2 * t].astype(F32), gather[2 * t + 1].astype(F32), low_lanes(32))
         tiles.append(jnp.concatenate([top, bottom], axis=0).astype(BF16))
     left = jnp.concatenate(tiles, axis=1)
-    loads[1].wait()
     for i in range(parts):
-        part_copy(i).wait()
         span = slice(i * DEPTH, (i + 1) * DEPTH)
         update = lax.dot_general(left, basis[span, :], (((1,), (1,)), ((), ())), preferred_element_type=F32)
         new_weight[:, span] = (weight[:, span].astype(F32) - step_size * update).astype(BF16)
-        out_copy(i).start()
-    for copy in loads[2:]:
+        stores.append(pltpu.make_async_copy(new_weight.at[:, span], weight_out.at[:, span], store_sem.at[2 + i]))
+        stores[-1].start()
+    for k in range(1, n_mp):
+        g_copy(k).wait_send()
+    for copy in stores:
         copy.wait()
-    new_moment[...] = beta_first * moment[...] + (1.0 - beta_first) * grad[...]
-    new_second[...] = beta_second * second[...] + (1.0 - beta_second) * grad[...] * grad[...]
-    stores = [
-        pltpu.make_async_copy(new_moment, moment_out, store_sem.at[0]),
-        pltpu.make_async_copy(new_second, second_out, store_sem.at[1]),
-    ]
-    for copy in stores:
+
+
+def copy_kernel(*refs):
+    count = (len(refs) - 1) // 2
+    copies = [pltpu.make_async_copy(refs[i], refs[count + i], refs[-1].at[i]) for i in range(count)]
+    for copy in copies:
         copy.start()
-    for i in range(parts):
-        out_copy(i).wait()
-    for copy in stores:
+    for copy in copies:
         copy.wait()
 
 
@@ -366,9 +333,8 @@
     cot = cotangent.reshape(micro * tokens, cotangent.shape[2])
     units, rank = subspace_basis.shape
     dma = pltpu.SemaphoreType.DMA
-    n = side - 1
     m = n_mp - 1
-    block = (2, HALF, 128)
+    n2 = 2 * side - 1
     plane = (side, HALF, 128)
     axis_recv = [
         pltpu.VMEM((2, 2) + plane, BF16),
@@ -380,9 +346,12 @@
         pltpu.VMEM(act.shape, BF16),
         pltpu.VMEM(cot.shape, BF16),
         pltpu.VMEM(subspace_basis.shape, BF16),
+        pltpu.VMEM(weight.shape, BF16),
         pltpu.VMEM(moment.shape, F32),
         pltpu.VMEM(second.shape, F32),
+        pltpu.VMEM(weight.shape, BF16),
         pltpu.VMEM(moment.shape, F32),
+        pltpu.VMEM(second.shape, F32),
         pltpu.VMEM((micro * tokens, rank), F32),
         pltpu.VMEM((n_mp, tokens, 128), BF16),
         pltpu.VMEM((m, tokens, 128), BF16),
@@ -391,61 +360,39 @@
         pltpu.VMEM((side, 2) + plane, BF16),
         *axis_recv,
         *axis_recv,
-        pltpu.VMEM((side,) + block, BF16),
-        pltpu.VMEM((side,) + block, BF16),
-        pltpu.VMEM((n,) + block, BF16),
-        pltpu.VMEM((n,) + block, BF16),
-        pltpu.VMEM((2, 32, 128), F32),
-        pltpu.VMEM((32, 128), F32),
+        pltpu.VMEM((side, 2, HALF, 128), BF16),
+        pltpu.VMEM((side, 2, HALF, 128), BF16),
+        pltpu.VMEM((n2, HALF, 128), BF16),
+        pltpu.VMEM((n2, HALF, 128), BF16),
         pltpu.VMEM((n_mp, 32, 128), BF16),
-        dma((3,)),
+        dma((4,)),
         dma((2, units // DEPTH)),
-        dma((2,)),
+        dma((2 + units // DEPTH,)),
         dma((m,)), dma((m,)),
         dma((4, 2)), dma((4, 2)), dma((4, 2)), dma((4, 2)),
-        dma((n,)), dma((n,)), dma((n,)), dma((n,)),
-        dma(()), dma(()),
+        dma((n2,)), dma((n2,)), dma((n2,)), dma((n2,)),
         dma((m,)), dma((m,)),
     ]
     hbm = pl.BlockSpec(memory_space=pltpu.HBM)
-    gathered, grad = pl.pallas_call(
-        functools.partial(gradient_kernel, side, n_mp),
-        out_shape=(
-            jax.ShapeDtypeStruct((n_mp, 32, 128), BF16),
-            jax.ShapeDtypeStruct(moment.shape, F32),
-        ),
-        in_specs=[hbm] * 5,
-        out_specs=(hbm,) * 2,
+    shapes = tuple(jax.ShapeDtypeStruct(a.shape, a.dtype) for a in (weight, moment, second))
+    results = pl.pallas_call(
+        functools.partial(step_kernel, side, n_mp),
+        out_shape=shapes,
+        in_specs=[hbm] * 6,
+        out_specs=(hbm,) * 3,
         scratch_shapes=scratch,
         compiler_params=pltpu.CompilerParams(
-            collective_id=0, has_side_effects=True, vmem_limit_bytes=60 * 1024 * 1024
+            collective_id=0, has_side_effects=True, vmem_limit_bytes=VMEM
         ),
-    )(act, cot, subspace_basis, moment, second)
+    )(act, cot, subspace_basis, weight, moment, second)
     return pl.pallas_call(
-        functools.partial(weight_kernel, n_mp),
-        out_shape=(
-            jax.ShapeDtypeStruct(weight.shape, BF16),
-            jax.ShapeDtypeStruct(moment.shape, F32),
-            jax.ShapeDtypeStruct(second.shape, F32),
-        ),
-        in_specs=[hbm] * 6,
+        copy_kernel,
+        out_shape=shapes,
+        in_specs=[hbm] * 3,
         out_specs=(hbm,) * 3,
-        scratch_shapes=[
-            pltpu.VMEM((n_mp, 32, 128), BF16),
-            pltpu.VMEM(moment.shape, F32),
-            pltpu.VMEM(subspace_basis.shape, BF16),
-            pltpu.VMEM(weight.shape, BF16),
-            pltpu.VMEM(moment.shape, F32),
-            pltpu.VMEM(second.shape, F32),
-            pltpu.VMEM(weight.shape, BF16),
-            pltpu.VMEM(moment.shape, F32),
-            pltpu.VMEM(second.shape, F32),
-            dma((5,)),
-            dma((2, units // DEPTH)),
-            dma((2,)),
-        ],
-        compiler_params=pltpu.CompilerParams(vmem_limit_bytes=60 * 1024 * 1024),
-    )(gathered, grad, subspace_basis, weight, moment, second)
+        scratch_shapes=[dma((3,))],
+        compiler_params=pltpu.CompilerParams(vmem_limit_bytes=VMEM),
+    )(*results)
 
 
 def solution(mesh):

time: 61.2 us -> 72.8 us (1.19)
  Pallas kernels: 60.4 us -> 72 us
    pallas_call x2, Pallas kernels: 60.4 us -> 72 us  [the longest x1 55 us: shards(): pl.pallas_call(functools.partial(step_kernel, side, n_mp), out_shape=shap...]
where the time goes in v3:
time: 72.8 us; the launch traced here: 72.7 us
  Pallas kernels  72 us (99%)
    pallas_call x1, Pallas kernels, shards(): pl.pallas_call(functools.partial(step_kernel, side, n_mp), out_shape=shap...  55 us
    pallas_call x1, Pallas kernels, shards(): pl.pallas_call(copy_kernel, out_shape=shapes, in_specs=[hbm] * 3, out_spe...  17 us

profile of v3, /device:TPU:1, one launch (start us, length us, event | category | flops | bytes accessed | tf_op | source)
XLA Modules:
  0.0 72.7 jit_solution(2129416548441887913)
XLA Ops:
  0.6 55.0 %shard_map.85 = (bf16[64,3584]{1,0:T(8,128)(2,1)}, f32[64,64]{1,0:T(8,128)}, f32[64,64]{1,0:T(8,128)}) custom-call(bf16[224,8192]{1,0:T(8,128)(2,1)} %bitcast.2, bf16[224,3584]{1,0:T(8,128)(2,1)} %bitcast.3, bf16[3584,512]{1,0:T(8,128)(2,1)} %basis_hbm.1, bf16[64,3584]{1,0:T(8,128)(2,1)} %weight_hbm.1, f32[64,64]{1,0:T(8,128)} %moment_hbm.1, f32[64,64]{1,0:T(8,128)} %second_hbm.1), custom_call_target="tpu_custom_call" | custom-call | tf_op jit(solution)/shard_map/pallas_call | solution.py:378
  55.7 17.0 %shard_map.86 = (bf16[64,3584]{1,0:T(8,128)(2,1)}, f32[64,64]{1,0:T(8,128)}, f32[64,64]{1,0:T(8,128)}) custom-call(bf16[64,3584]{1,0:T(8,128)(2,1)} %get-tuple-element.6.refs_0_, f32[64,64]{1,0:T(8,128)} %get-tuple-element.7.refs_1_, f32[64,64]{1,0:T(8,128)} %get-tuple-element.8.refs_2_), custom_call_target="tpu_custom_call" | custom-call | tf_op jit(solution)/shard_map/pallas_call | solution.py:388

commit v4 on v3

--- a/solution.py
+++ b/solution.py
@@ -39,7 +39,7 @@
 def step_kernel(
     side, n_mp, act_hbm, cot_hbm, basis_hbm, weight_hbm, moment_hbm, second_hbm,
     weight_out, moment_out, second_out,
-    act, cot, basis, weight, moment, second, new_weight, new_moment, new_second,
+    act, cot, basis, weight, moment, second, half_weight, new_weight, new_moment, new_second,
     partial, mp_send, mp_recv, rows_t, y_send, z_send,
     y_recv1, y_recv2, y_recv3, y_recv4, z_recv1, z_recv2, z_recv3, z_recv4,
     zz_send, yy_send, zz_recv, yy_recv, gather,
@@ -282,10 +282,6 @@
     def g_copy(k):
         return remote(gather.at[mp], gather.at[mp], g_ss.at[k - 1], g_rs.at[k - 1], mp_peer(k))
 
-    def g_arrival(k):
-        slot = lax.rem(mp + n_mp - k, n_mp)
-        return remote(gather.at[slot], gather.at[slot], g_ss.at[k - 1], g_rs.at[k - 1], mp_peer(k))
-
     for k in far_first(n_mp):
         g_copy(k).start()
     stores = [
@@ -299,31 +295,58 @@
         for copy in copies:
             copy.wait_send()
     loads[3].wait()
-    for k in reversed(far_first(n_mp)):
-        g_arrival(k).wait_recv()
-    tiles = []
-    for t in range(n_mp // 2):
-        top, bottom = halves(gather[2 * t].astype(F32), gather[2 * t + 1].astype(F32), low_lanes(32))
-        tiles.append(jnp.concatenate([top, bottom], axis=0).astype(BF16))
-    left = jnp.concatenate(tiles, axis=1)
-    for i in range(parts):
-        span = slice(i * DEPTH, (i + 1) * DEPTH)
-        update = lax.dot_general(left, basis[span, :], (((1,), (1,)), ((), ())), preferred_element_type=F32)
-        new_weight[:, span] = (weight[:, span].astype(F32) - step_size * update).astype(BF16)
-        stores.append(pltpu.make_async_copy(new_weight.at[:, span], weight_out.at[:, span], store_sem.at[2 + i]))
-        stores[-1].start()
+
+    def pair_of(steps):
+        return lax.rem(mp // 2 + steps, n_mp // 2)
+
+    def pair_tile(pair):
+        top, bottom = halves(gather[2 * pair].astype(F32), gather[2 * pair + 1].astype(F32), low_lanes(32))
+        return jnp.concatenate([top, bottom], axis=0).astype(BF16)
+
+    def arrivals(pairs):
+        for steps in pairs:
+            for core in range(2):
+                slot = 2 * pair_of(steps) + core
+                k = lax.rem(mp + n_mp - slot, n_mp)
+
+                @pl.when(k > 0)
+                def _():
+                    remote(gather.at[slot], gather.at[slot], g_ss.at[0], g_rs.at[k - 1], mp_peer(1)).wait_recv()
+
+    pairs = n_mp // 2
+    near_pairs, far_pairs = (0, 1), (pairs - 1, pairs - 2)
+    for stage, group in enumerate((near_pairs, far_pairs)):
+        arrivals(group)
+        left = jnp.concatenate([pair_tile(pair_of(steps)) for steps in group], axis=1)
+        columns = [pl.ds(pl.multiple_of(pair_of(steps) * 128, 128), 128) for steps in group]
+        for i in range(parts):
+            span = slice(i * DEPTH, (i + 1) * DEPTH)
+            right = jnp.concatenate([basis[span, cols] for cols in columns], axis=1)
+            update = lax.dot_general(left, right, (((1,), (1,)), ((), ())), preferred_element_type=F32)
+            if stage == 0:
+                half_weight[:, span] = weight[:, span].astype(F32) - step_size * update
+            else:
+                new_weight[:, span] = (half_weight[:, span] - step_size * update).astype(BF16)
+                stores.append(pltpu.make_async_copy(new_weight.at[:, span], weight_out.at[:, span], store_sem.at[2 + i]))
+                stores[-1].start()
     for k in range(1, n_mp):
         g_copy(k).wait_send()
     for copy in stores:
         copy.wait()
 
 
-def copy_kernel(*refs):
-    count = (len(refs) - 1) // 2
-    copies = [pltpu.make_async_copy(refs[i], refs[count + i], refs[-1].at[i]) for i in range(count)]
-    for copy in copies:
+def copy_kernel(weight_in, moment_in, second_in, weight_out, moment_out, second_out, weight, moment, second, load_sem, store_sem):
+    rows = [pl.ds(start, HALF) for start in range(0, OWN, HALF)]
+    pieces = [(weight_in.at[r], weight.at[r], weight_out.at[r]) for r in rows]
+    pieces += [(moment_in, moment, moment_out), (second_in, second, second_out)]
+    loads = [pltpu.make_async_copy(a, b, load_sem.at[i]) for i, (a, b, _) in enumerate(pieces)]
+    stores = [pltpu.make_async_copy(b, c, store_sem.at[i]) for i, (_, b, c) in enumerate(pieces)]
+    for copy in loads:
         copy.start()
-    for copy in copies:
+    for load, store in zip(loads, stores):
+        load.wait()
+        store.start()
+    for copy in stores:
         copy.wait()
 
 
@@ -349,6 +372,7 @@
         pltpu.VMEM(weight.shape, BF16),
         pltpu.VMEM(moment.shape, F32),
         pltpu.VMEM(second.shape, F32),
+        pltpu.VMEM(weight.shape, F32),
         pltpu.VMEM(weight.shape, BF16),
         pltpu.VMEM(moment.shape, F32),
         pltpu.VMEM(second.shape, F32),
@@ -390,7 +414,8 @@
         out_shape=shapes,
         in_specs=[hbm] * 3,
         out_specs=(hbm,) * 3,
-        scratch_shapes=[dma((3,))],
+        scratch_shapes=[pltpu.VMEM(a.shape, a.dtype) for a in shapes]
+        + [dma((2 + OWN // HALF,)), dma((2 + OWN // HALF,))],
         compiler_params=pltpu.CompilerParams(vmem_limit_bytes=VMEM),
     )(*results)
 

time: 72.8 us -> 57.7 us (0.79)
  Pallas kernels: 72 us -> 56.9 us
    pallas_call x1, Pallas kernels: 17 us -> 1.83 us  [shards(): pl.pallas_call(copy_kernel, out_shape=shapes, in_specs=[hbm] * 3, out_spe...]
where the time goes in v4:
time: 57.7 us; the launch traced here: 57.5 us
  Pallas kernels  56.9 us (99%)
  between operations  0.64 us (1%)
    pallas_call x1, Pallas kernels, shards(): pl.pallas_call(functools.partial(step_kernel, side, n_mp), out_shape=shap...  55 us
    pallas_call x1, Pallas kernels, shards(): pl.pallas_call(copy_kernel, out_shape=shapes, in_specs=[hbm] * 3, out_spe...  1.83 us

profile of v4, /device:TPU:1, one launch (start us, length us, event | category | flops | bytes accessed | tf_op | source)
XLA Modules:
  0.0 57.5 jit_solution(1398310112913143170)
XLA Ops:
  0.6 55.0 %shard_map.85 = (bf16[64,3584]{1,0:T(8,128)(2,1)}, f32[64,64]{1,0:T(8,128)}, f32[64,64]{1,0:T(8,128)}) custom-call(bf16[224,8192]{1,0:T(8,128)(2,1)} %bitcast.2, bf16[224,3584]{1,0:T(8,128)(2,1)} %bitcast.3, bf16[3584,512]{1,0:T(8,128)(2,1)} %basis_hbm.1, bf16[64,3584]{1,0:T(8,128)(2,1)} %weight_hbm.1, f32[64,64]{1,0:T(8,128)} %moment_hbm.1, f32[64,64]{1,0:T(8,128)} %second_hbm.1), custom_call_target="tpu_custom_call" | custom-call | tf_op jit(solution)/shard_map/pallas_call | solution.py:402
  55.7 1.8 %shard_map.86 = (bf16[64,3584]{1,0:T(8,128)(2,1)}, f32[64,64]{1,0:T(8,128)}, f32[64,64]{1,0:T(8,128)}) custom-call(bf16[64,3584]{1,0:T(8,128)(2,1)} %get-tuple-element.6.weight_in, f32[64,64]{1,0:T(8,128)} %get-tuple-element.7.moment_in, f32[64,64]{1,0:T(8,128)} %get-tuple-element.8.second_in), custom_call_target="tpu_custom_call" | custom-call | tf_op jit(solution)/shard_map/pallas_call | solution.py:412

commit v5 on v4

--- a/solution.py
+++ b/solution.py
@@ -84,7 +84,19 @@
             pltpu.make_async_copy(cot_hbm.at[:, span], cot.at[:, span], part_sem.at[1, i]),
         )
 
-    for i in range(parts):
+    early = parts // 2
+    for i in range(early):
+        for copy in part_copies(i):
+            copy.start()
+
+    barrier = pltpu.get_barrier_semaphore()
+    peers = [xz_peer(k, flip) for flip in range(2) for k in range(1, side)]
+    peers += [xy_peer(k, flip) for flip in (1, 0) for k in range(1 - flip, side)]
+    peers += [mp_peer(k) for k in range(1, n_mp)]
+    for peer in peers:
+        pl.semaphore_signal(barrier, inc=1, device_id=peer, device_id_type=MESH_ID)
+
+    for i in range(early, parts):
         for copy in part_copies(i):
             copy.start()
     loads = [
@@ -96,15 +108,6 @@
     for copy in loads:
         copy.start()
 
-    barrier = pltpu.get_barrier_semaphore()
-    for k in range(1, n_mp):
-        pl.semaphore_signal(barrier, inc=1, device_id=mp_peer(k), device_id_type=MESH_ID)
-    for flip in range(2):
-        for k in range(1, side):
-            pl.semaphore_signal(barrier, inc=1, device_id=xy_peer(k, flip), device_id_type=MESH_ID)
-            pl.semaphore_signal(barrier, inc=1, device_id=xz_peer(k, flip), device_id_type=MESH_ID)
-    pl.semaphore_signal(barrier, inc=1, device_id=xy_peer(0, 1), device_id_type=MESH_ID)
-
     for i in range(parts):
         for copy in part_copies(i):
             copy.wait()
@@ -121,7 +124,7 @@
         mp_send[2 * t] = first.astype(BF16)
         mp_send[2 * t + 1] = other.astype(BF16)
 
-    pl.semaphore_wait(barrier, n_mp - 1 + 4 * (side - 1) + 1)
+    pl.semaphore_wait(barrier, len(peers))
 
     def mp_copy(k):
         return remote(

time: 57.7 us -> 58.2 us (level)
  no operation moved by 1% of the time
where the time goes in v5:
time: 58.2 us; the launch traced here: 58 us
  Pallas kernels  57.4 us (99%)
  between operations  0.64 us (1%)
    pallas_call x1, Pallas kernels, shards(): pl.pallas_call(functools.partial(step_kernel, side, n_mp), out_shape=shap...  55.6 us
    pallas_call x1, Pallas kernels, shards(): pl.pallas_call(copy_kernel, out_shape=shapes, in_specs=[hbm] * 3, out_spe...  1.83 us

profile of v5, /device:TPU:1, one launch (start us, length us, event | category | flops | bytes accessed | tf_op | source)
XLA Modules:
  0.0 58.0 jit_solution(15655995689460323665)
XLA Ops:
  0.6 55.6 %shard_map.85 = (bf16[64,3584]{1,0:T(8,128)(2,1)}, f32[64,64]{1,0:T(8,128)}, f32[64,64]{1,0:T(8,128)}) custom-call(bf16[224,8192]{1,0:T(8,128)(2,1)} %bitcast.2, bf16[224,3584]{1,0:T(8,128)(2,1)} %bitcast.3, bf16[3584,512]{1,0:T(8,128)(2,1)} %basis_hbm.1, bf16[64,3584]{1,0:T(8,128)(2,1)} %weight_hbm.1, f32[64,64]{1,0:T(8,128)} %moment_hbm.1, f32[64,64]{1,0:T(8,128)} %second_hbm.1), custom_call_target="tpu_custom_call" | custom-call | tf_op jit(solution)/shard_map/pallas_call | solution.py:405
  56.2 1.8 %shard_map.86 = (bf16[64,3584]{1,0:T(8,128)(2,1)}, f32[64,64]{1,0:T(8,128)}, f32[64,64]{1,0:T(8,128)}) custom-call(bf16[64,3584]{1,0:T(8,128)(2,1)} %get-tuple-element.6.weight_in, f32[64,64]{1,0:T(8,128)} %get-tuple-element.7.moment_in, f32[64,64]{1,0:T(8,128)} %get-tuple-element.8.second_in), custom_call_target="tpu_custom_call" | custom-call | tf_op jit(solution)/shard_map/pallas_call | solution.py:415
